TPU v7x, 32 devices: a whole 2x2x4 slice. The times are simulated.
32 devices in a mesh: groups: 1, expert: 4 (over z), replica: 8 (over y, x, core).
Axes of the slice: x: 2, y: 2, z: 4, core: 2. Of those that a mesh axis runs over, the one named last changes fastest.
Arguments:
- beam_rows: bfloat16 [32, 4096], P(('groups', 'expert', 'replica')), may hold values from -6 to 6
- norm_gain: float32 [4096], replicated, may hold values from 0.1 to 1.9
- router: bfloat16 [4096, 4], replicated, may hold values from -0.09375 to 0.09375
- gate_proj: bfloat16 [4, 4096, 1024], P('expert', None, 'replica'), may hold values from -0.09375 to 0.09375
- up_proj: bfloat16 [4, 4096, 1024], P('expert', None, 'replica'), may hold values from -0.09375 to 0.09375
- down_proj: bfloat16 [4, 1024, 4096], P('expert', 'replica'), may hold values from -0.1875 to 0.1875
- routes: int32 [32, 2], P(('groups', 'expert')), may hold values from 0 to 3, all different within a row; in each aligned block of 8 rows (0 to 7, 8 to 15, ...) at most 8 rows name the same one
Outputs:
- expert_out: bfloat16 [32, 4096], P(('groups', 'expert', 'replica'))
Inputs may be any that keep to these rules, and one draw needn't show every extreme that they name: `routes`: each row names 2 different experts. Among the 8 rows of one index of expert (rows k * 8 to (k + 1) * 8 - 1) at most 8 rows name one expert, and in some such block one expert is named by exactly 8 rows.
All inputs are finite; a program needn't handle non-finite values.
Results may differ from a plain program's by a relative error of at most 0.0057.
Values may be sent and summed in bfloat16 or wider, within the bound.
A program may use at most 64 MiB of HBM per device.

v0:
```python
import jax
import jax.numpy as jnp
from jax import lax
from jax.sharding import PartitionSpec as P

ROUTE_SCALE = 2.5


def shifted(block, axis, distance):
    devices = range(lax.axis_size(axis))
    route = [((i - distance) % len(devices), i) for i in devices]
    return lax.ppermute(block, axis, route)


def rms_rows(beam_rows, norm_gain):
    values = beam_rows.astype(jnp.float32)
    inverse_rms = lax.rsqrt(jnp.mean(values * values, axis=-1, keepdims=True) + 1e-06)
    return (values * inverse_rms * norm_gain).astype(jnp.bfloat16)


def route_weights(normed, router, routes):
    expert_count = router.shape[1]
    logits = jnp.dot(normed, router, preferred_element_type=jnp.float32)
    members = jnp.sum(
        (routes[:, :, None] == jnp.arange(expert_count, dtype=jnp.int32)[None, None, :]).astype(
            jnp.float32
        ),
        axis=1,
    )
    chosen = jax.nn.sigmoid(logits) * members
    return (ROUTE_SCALE * chosen / jnp.sum(chosen, axis=1, keepdims=True), members)


def expert_part(normed, gate_slice, up_slice, down_slice):
    gate_act = jnp.dot(normed, gate_slice, preferred_element_type=jnp.float32)
    up_act = jnp.dot(normed, up_slice, preferred_element_type=jnp.float32)
    hidden = (jax.nn.silu(gate_act) * up_act).astype(jnp.bfloat16)
    return jnp.dot(hidden, down_slice, preferred_element_type=jnp.float32)


def on_device(beam_rows, norm_gain, router, gate_proj, up_proj, down_proj, routes):
    normed = rms_rows(beam_rows, norm_gain)
    row_block = lax.all_gather(normed, "replica", axis=0, tiled=True)
    combine_weights, members = route_weights(row_block, router, routes)
    resident = gate_proj.shape[0]
    first_expert = lax.axis_index("expert") * resident

    def apply_local(running, visiting, carried):
        column = lax.dynamic_slice_in_dim(carried, first_expert + 0, 1, 1)
        running = running + column * expert_part(visiting, gate_proj[0], up_proj[0], down_proj[0])
        return running

    hop_count = lax.axis_size("expert")

    def cycle_hop(cycle_step, cycle_state):
        visiting, running, carried = cycle_state
        running = apply_local(running, visiting, carried)
        visiting = shifted(visiting, "expert", 1)
        running, carried = shifted((running, carried), "expert", 1)
        return (visiting, running, carried)

    empty_sums = jnp.zeros(row_block.shape, jnp.float32)
    visiting, running, carried = lax.fori_loop(
        0, hop_count - 1, cycle_hop, (row_block, empty_sums, combine_weights)
    )
    running = apply_local(running, visiting, carried)
    combined = shifted(running, "expert", 1)
    row_share = lax.psum_scatter(combined, "replica", scatter_dimension=0, tiled=True)
    return (beam_rows.astype(jnp.float32) + row_share).astype(jnp.bfloat16)


def solution(mesh):
    placed = (
        P(("groups", "expert", "replica"), None),
        P(),
        P(),
        P("expert", None, "replica"),
        P("expert", None, "replica"),
        P("expert", "replica", None),
        P(("groups", "expert"), None),
    )
    return jax.shard_map(
        on_device,
        mesh=mesh,
        in_specs=placed,
        out_specs=P(("groups", "expert", "replica"), None),
        check_vma=False,
    )
```

profile of v0, /device:TPU:0, one launch (start us, length us, event | category | flops | bytes accessed | tf_op | source)
XLA Modules:
  0.0 125.2 jit_solution(15646585544241775845)
XLA Ops:
  6.5 1.4 %multiply_reduce_fusion = f32[]{:T(128)} fusion(bf16[1,4096]{1,0:T(2,128)(2,1)} %param.9), kind=kLoop, calls=%fused_computation.33 | loop fusion | flops 12287 | bytes 8196 | tf_op jit(solution)/shard_map/reduce_sum | solution.py:17
  8.6 10.7 %all-gather = bf16[8,1,4096]{2,1,0:T(2,128)(2,1)S(1)} all-gather(bf16[1,1,4096]{2,1,0:T(2,128)(2,1)S(1)} %convert_bitcast_fusion), channel_id=1, replica_groups=mesh['groups'=1,'expert'=4,'replica'=8] {'replica'}, dimensions={0}, use_global_device_ids=true | all-gather | bytes 73728 | tf_op jit(solution)/shard_map/all_gather | solution.py:43
  19.3 0.1 copy.13
  19.4 0.6 copy-done.6
  20.0 0.2 fusion.33
  20.2 34.9 %while.16 = (s32[]{:T(128)}, bf16[8,4096]{1,0:T(8,128)(2,1)S(1)}, f32[8,4096]{1,0:T(8,128)S(1)}, f32[8,4]{0,1:T(4,128)S(1)}, s32[]{:T(128)}, /*index=5*/bf16[1,4...) while((s32[]{:T(128)}, bf16[8,4096]{1,0:T(8,128)(2,1)S(1)}, ...), condition=%wide.region_4.5_spmd, body=%wide.region_3.4_spmd.sunk | while | flops 25237504 | bytes 8660053 | solution.py:63
  20.3 1.6 %fusion.52 = f32[8,128]{1,0:T(8,128)S(1)} fusion(bf16[8,4096]{1,0:T(8,128)(2,1)S(1)} %copy.19, bf16[1,4096,128]{2,1,0:T(8,128)(2,1)} %get-tuple-element.196), kind=kOutput, calls=%fused_computation.6.clone.1 | convolution fusion | flops 8388608 | bytes 1118208 | tf_op jit(solution)/shard_map/while/body/eval_jaxpr/dot_general | solution.py:35
  21.8 1.7 %fusion.53 = f32[8,4096]{1,0:T(8,128)S(1)} fusion(f32[8,4096]{1,0:T(8,128)S(1)} %get-tuple-element.184, bf16[8,4096]{1,0:T(8,128)(2,1)S(1)} %copy.19, bf16[1,128,4096]{2,1,0:T(8,128)(2,1)} %get-tuple-element.198, bf16[1,4096,128]{2,1,0:T(8,128)(2,1)S(1)} %copy-done.1, f32[8]{0:T(128)S(1)} %dynamic-slice_bitcast_fusion.3, f32[8,128]{1,0:T(8,128)S(1)} %fusion.52), kind=kOutput, calls=%fused_computation.1.clone.1 | convolution fusion | flops 16848896 | bytes 2428960 | tf_op jit(solution)/shard_map/while/body/eval_jaxpr/dot_general | solution.py:38
  23.5 1.6 %collective-permute-start.1 = (f32[8,4096]{1,0:T(8,128)S(1)}, f32[8,4096]{1,0:T(8,128)S(1)}, u32[]{:S(2)}, u32[]{:S(2)}) collective-permute-start(f32[8,4096]{1,0:T(8,128)S(1)} %fusion.53), channel_id=1, source_target_pairs={{24,0},{0,8},{8,16},{16,24},{25,1},{1,9},{9,17},{17,25},{26,2},{2,... | collective-permute-start | bytes 393224 | tf_op jit(solution)/shard_map/while/body/eval_jaxpr/ppermute | solution.py:12
  25.2 1.6 %collective-permute-start = (bf16[8,4096]{1,0:T(8,128)(2,1)S(1)}, bf16[8,4096]{1,0:T(8,128)(2,1)S(1)}, u32[]{:S(2)}, u32[]{:S(2)}) collective-permute-start(bf16[8,4096]{1,0:T(8,128)(2,1)S(1)} %copy.19), channel_id=1, source_target_pairs={{24,0},{0,8},{8,16},{16,24},{25,1},{1,9},{9,17},{17,25},{26,2},{2,... | collective-permute-start | bytes 196616 | tf_op jit(solution)/shard_map/while/body/eval_jaxpr/ppermute | solution.py:12
  26.7 1.6 %collective-permute-start.2 = (f32[8,4]{0,1:T(4,128)S(1)}, f32[8,4]{0,1:T(4,128)S(1)}, u32[]{:S(2)}, u32[]{:S(2)}) collective-permute-start(f32[8,4]{0,1:T(4,128)S(1)} %copy.21), channel_id=1, source_target_pairs={{24,0},{0,8},{8,16},{16,24},{25,1},{1,9},{9,17},{17,25},{26,2},{2,... | collective-permute-start | bytes 392 | tf_op jit(solution)/shard_map/while/body/eval_jaxpr/ppermute | solution.py:12
  28.3 4.3 %collective-permute-done.2 = f32[8,4]{0,1:T(4,128)S(1)} collective-permute-done((f32[8,4]{0,1:T(4,128)S(1)}, f32[8,4]{0,1:T(4,128)S(1)}, u32[]{:S(2)}, u32[]{:S(2)}) %collective-permute-start.2) | collective-permute-done | bytes 160 | tf_op jit(solution)/shard_map/while/body/eval_jaxpr/ppermute | solution.py:12
  32.7 1.6 %fusion.52 = f32[8,128]{1,0:T(8,128)S(1)} fusion(bf16[8,4096]{1,0:T(8,128)(2,1)S(1)} %copy.19, bf16[1,4096,128]{2,1,0:T(8,128)(2,1)} %get-tuple-element.196), kind=kOutput, calls=%fused_computation.6.clone.1 | convolution fusion | flops 8388608 | bytes 1118208 | tf_op jit(solution)/shard_map/while/body/eval_jaxpr/dot_general | solution.py:35
  34.2 1.7 %fusion.53 = f32[8,4096]{1,0:T(8,128)S(1)} fusion(f32[8,4096]{1,0:T(8,128)S(1)} %get-tuple-element.184, bf16[8,4096]{1,0:T(8,128)(2,1)S(1)} %copy.19, bf16[1,128,4096]{2,1,0:T(8,128)(2,1)} %get-tuple-element.198, bf16[1,4096,128]{2,1,0:T(8,128)(2,1)S(1)} %copy-done.1, f32[8]{0:T(128)S(1)} %dynamic-slice_bitcast_fusion.3, f32[8,128]{1,0:T(8,128)S(1)} %fusion.52), kind=kOutput, calls=%fused_computation.1.clone.1 | convolution fusion | flops 16848896 | bytes 2428960 | tf_op jit(solution)/shard_map/while/body/eval_jaxpr/dot_general | solution.py:38
  35.9 0.0 collective-permute-start.1
  36.0 1.3 %collective-permute-start = (bf16[8,4096]{1,0:T(8,128)(2,1)S(1)}, bf16[8,4096]{1,0:T(8,128)(2,1)S(1)}, u32[]{:S(2)}, u32[]{:S(2)}) collective-permute-start(bf16[8,4096]{1,0:T(8,128)(2,1)S(1)} %copy.19), channel_id=1, source_target_pairs={{24,0},{0,8},{8,16},{16,24},{25,1},{1,9},{9,17},{17,25},{26,2},{2,... | collective-permute-start | bytes 196616 | tf_op jit(solution)/shard_map/while/body/eval_jaxpr/ppermute | solution.py:12
  37.3 1.6 %collective-permute-start.2 = (f32[8,4]{0,1:T(4,128)S(1)}, f32[8,4]{0,1:T(4,128)S(1)}, u32[]{:S(2)}, u32[]{:S(2)}) collective-permute-start(f32[8,4]{0,1:T(4,128)S(1)} %copy.21), channel_id=1, source_target_pairs={{24,0},{0,8},{8,16},{16,24},{25,1},{1,9},{9,17},{17,25},{26,2},{2,... | collective-permute-start | bytes 392 | tf_op jit(solution)/shard_map/while/body/eval_jaxpr/ppermute | solution.py:12
  38.9 5.4 %collective-permute-done.2 = f32[8,4]{0,1:T(4,128)S(1)} collective-permute-done((f32[8,4]{0,1:T(4,128)S(1)}, f32[8,4]{0,1:T(4,128)S(1)}, u32[]{:S(2)}, u32[]{:S(2)}) %collective-permute-start.2) | collective-permute-done | bytes 160 | tf_op jit(solution)/shard_map/while/body/eval_jaxpr/ppermute | solution.py:12
  44.3 1.6 %fusion.52 = f32[8,128]{1,0:T(8,128)S(1)} fusion(bf16[8,4096]{1,0:T(8,128)(2,1)S(1)} %copy.19, bf16[1,4096,128]{2,1,0:T(8,128)(2,1)} %get-tuple-element.196), kind=kOutput, calls=%fused_computation.6.clone.1 | convolution fusion | flops 8388608 | bytes 1118208 | tf_op jit(solution)/shard_map/while/body/eval_jaxpr/dot_general | solution.py:35
  45.9 1.7 %fusion.53 = f32[8,4096]{1,0:T(8,128)S(1)} fusion(f32[8,4096]{1,0:T(8,128)S(1)} %get-tuple-element.184, bf16[8,4096]{1,0:T(8,128)(2,1)S(1)} %copy.19, bf16[1,128,4096]{2,1,0:T(8,128)(2,1)} %get-tuple-element.198, bf16[1,4096,128]{2,1,0:T(8,128)(2,1)S(1)} %copy-done.1, f32[8]{0:T(128)S(1)} %dynamic-slice_bitcast_fusion.3, f32[8,128]{1,0:T(8,128)S(1)} %fusion.52), kind=kOutput, calls=%fused_computation.1.clone.1 | convolution fusion | flops 16848896 | bytes 2428960 | tf_op jit(solution)/shard_map/while/body/eval_jaxpr/dot_general | solution.py:38
  47.6 0.3 collective-permute-start
  47.9 0.7 collective-permute-start.2
  48.6 6.5 %collective-permute-done.2 = f32[8,4]{0,1:T(4,128)S(1)} collective-permute-done((f32[8,4]{0,1:T(4,128)S(1)}, f32[8,4]{0,1:T(4,128)S(1)}, u32[]{:S(2)}, u32[]{:S(2)}) %collective-permute-start.2) | collective-permute-done | bytes 160 | tf_op jit(solution)/shard_map/while/body/eval_jaxpr/ppermute | solution.py:12
  55.1 1.6 %fusion.23 = f32[8,128]{1,0:T(8,128)S(1)} fusion(bf16[8,4096]{1,0:T(8,128)(2,1)S(1)} %get-tuple-element.105, bf16[1,4096,128]{2,1,0:T(8,128)(2,1)} %get-tuple-element.201), kind=kOutput, calls=%fused_computation.27 | convolution fusion | flops 8388608 | bytes 1118208 | tf_op jit(solution)/shard_map/dot_general | solution.py:35
  56.7 1.7 %fusion.14 = f32[8,4096]{1,0:T(8,128)S(1)} fusion(f32[8,4096]{1,0:T(8,128)S(1)} %get-tuple-element.103, bf16[8,4096]{1,0:T(8,128)(2,1)S(1)} %get-tuple-element.105, bf16[1,128,4096]{2,1,0:T(8,128)(2,1)} %get-tuple-element.203, bf16[1,4096,128]{2,1,0:T(8,128)(2,1)S(1)} %copy-done.2, f32[8]{0:T(128)S(1)} %dynamic-slice_bitcast_fusion.1, f32[8,128]{1,0:T(8,128)S(1)} %fusion.23), kind=kOutput, calls=%fused_computation.17 | convolution fusion | flops 16848896 | bytes 2428960 | tf_op jit(solution)/shard_map/dot_general | solution.py:38
  58.4 0.0 collective-permute-start.3
  58.4 6.8 %collective-permute-done.3 = f32[8,4096]{1,0:T(8,128)S(1)} collective-permute-done((f32[8,4096]{1,0:T(8,128)S(1)}, f32[8,4096]{1,0:T(8,128)S(1)}, u32[]{:S(2)}, u32[]{:S(2)}) %collective-permute-start.3) | collective-permute-done | bytes 131104 | tf_op jit(solution)/shard_map/ppermute | solution.py:12
  65.2 0.6 copy-done.4
  65.9 0.6 copy-done.7
  66.5 0.6 dynamic-slice
  67.1 49.1 %all-reduce.3.cloned.1.call-done = f32[8,4096]{1,0:T(8,128)} async-done(((f32[8,4096]{1,0:T(8,128)}), f32[8,4096]{1,0:T(8,128)}) %all-reduce.3.cloned.1.call-update) | async-done | bytes 131088
  116.2 2.2 %fusion.25 = bf16[1,4096]{1,0:T(2,128)(2,1)} fusion(f32[8,4096]{1,0:T(8,128)} %all-reduce.3.cloned.1.call-done, u32[]{:T(128)} %bitcast.10, bf16[1,4096]{1,0:T(2,128)(2,1)S(1)} %copy-done.3), kind=kLoop, calls=%fused_computation.31 | loop fusion | flops 12288 | bytes 32772 | tf_op jit(solution)/shard_map/convert_element_type | solution.py:69
  (40 shorter events, 0.2 us)
Async XLA Ops:
  6.5 13.5 %copy-start = (bf16[4096,4]{0,1:T(4,128)(2,1)S(1)}, bf16[4096,4]{0,1:T(4,128)(2,1)}, u32[]{:S(2)}) copy-start(bf16[4096,4]{0,1:T(4,128)(2,1)} %param.11) | copy-start | bytes 98308
  6.5 109.7 %all-reduce.3.cloned.1.call-start = ((), (), s32[]{:S(2)}) async-start(), calls=%async_computation | async-start | bytes 262144
  6.5 2.0 %copy-start.5 = (f32[4096]{0:T(1024)S(1)}, f32[4096]{0:T(1024)}, u32[]{:S(2)}) copy-start(f32[4096]{0:T(1024)} %param.10) | copy-start | bytes 49156
  6.5 2.0 %copy-start.3 = (bf16[1,4096]{1,0:T(2,128)(2,1)S(1)}, bf16[1,4096]{1,0:T(2,128)(2,1)}, u32[]{:S(2)}) copy-start(bf16[1,4096]{1,0:T(2,128)(2,1)} %param.9) | copy-start | bytes 24580
  19.3 0.7 copy-start.6
  20.2 1.6 %copy-start.1 = (bf16[1,4096,128]{2,1,0:T(8,128)(2,1)S(1)}, bf16[1,4096,128]{2,1,0:T(8,128)(2,1)}, u32[]{:S(2)}) copy-start(bf16[1,4096,128]{2,1,0:T(8,128)(2,1)} %get-tuple-element.197) | copy-start | bytes 3145732 | tf_op jit(solution)/shard_map/while
  23.5 9.1 %collective-permute-start.1 = (f32[8,4096]{1,0:T(8,128)S(1)}, f32[8,4096]{1,0:T(8,128)S(1)}, u32[]{:S(2)}, u32[]{:S(2)}) collective-permute-start(f32[8,4096]{1,0:T(8,128)S(1)} %fusion.53), channel_id=1, source_target_pairs={{24,0},{0,8},{8,16},{16,24},{25,1},{1,9},{9,17},{17,25},{26,2},{2,... | collective-permute-start | bytes 393224 | tf_op jit(solution)/shard_map/while/body/eval_jaxpr/ppermute | solution.py:12
  25.2 7.5 %collective-permute-start = (bf16[8,4096]{1,0:T(8,128)(2,1)S(1)}, bf16[8,4096]{1,0:T(8,128)(2,1)S(1)}, u32[]{:S(2)}, u32[]{:S(2)}) collective-permute-start(bf16[8,4096]{1,0:T(8,128)(2,1)S(1)} %copy.19), channel_id=1, source_target_pairs={{24,0},{0,8},{8,16},{16,24},{25,1},{1,9},{9,17},{17,25},{26,2},{2,... | collective-permute-start | bytes 196616 | tf_op jit(solution)/shard_map/while/body/eval_jaxpr/ppermute | solution.py:12
  26.7 5.9 %collective-permute-start.2 = (f32[8,4]{0,1:T(4,128)S(1)}, f32[8,4]{0,1:T(4,128)S(1)}, u32[]{:S(2)}, u32[]{:S(2)}) collective-permute-start(f32[8,4]{0,1:T(4,128)S(1)} %copy.21), channel_id=1, source_target_pairs={{24,0},{0,8},{8,16},{16,24},{25,1},{1,9},{9,17},{17,25},{26,2},{2,... | collective-permute-start | bytes 392 | tf_op jit(solution)/shard_map/while/body/eval_jaxpr/ppermute | solution.py:12
  32.6 1.6 %copy-start.1 = (bf16[1,4096,128]{2,1,0:T(8,128)(2,1)S(1)}, bf16[1,4096,128]{2,1,0:T(8,128)(2,1)}, u32[]{:S(2)}) copy-start(bf16[1,4096,128]{2,1,0:T(8,128)(2,1)} %get-tuple-element.197) | copy-start | bytes 3145732 | tf_op jit(solution)/shard_map/while
  35.9 8.3 %collective-permute-start.1 = (f32[8,4096]{1,0:T(8,128)S(1)}, f32[8,4096]{1,0:T(8,128)S(1)}, u32[]{:S(2)}, u32[]{:S(2)}) collective-permute-start(f32[8,4096]{1,0:T(8,128)S(1)} %fusion.53), channel_id=1, source_target_pairs={{24,0},{0,8},{8,16},{16,24},{25,1},{1,9},{9,17},{17,25},{26,2},{2,... | collective-permute-start | bytes 393224 | tf_op jit(solution)/shard_map/while/body/eval_jaxpr/ppermute | solution.py:12
  36.0 8.3 %collective-permute-start = (bf16[8,4096]{1,0:T(8,128)(2,1)S(1)}, bf16[8,4096]{1,0:T(8,128)(2,1)S(1)}, u32[]{:S(2)}, u32[]{:S(2)}) collective-permute-start(bf16[8,4096]{1,0:T(8,128)(2,1)S(1)} %copy.19), channel_id=1, source_target_pairs={{24,0},{0,8},{8,16},{16,24},{25,1},{1,9},{9,17},{17,25},{26,2},{2,... | collective-permute-start | bytes 196616 | tf_op jit(solution)/shard_map/while/body/eval_jaxpr/ppermute | solution.py:12
  37.3 7.0 %collective-permute-start.2 = (f32[8,4]{0,1:T(4,128)S(1)}, f32[8,4]{0,1:T(4,128)S(1)}, u32[]{:S(2)}, u32[]{:S(2)}) collective-permute-start(f32[8,4]{0,1:T(4,128)S(1)} %copy.21), channel_id=1, source_target_pairs={{24,0},{0,8},{8,16},{16,24},{25,1},{1,9},{9,17},{17,25},{26,2},{2,... | collective-permute-start | bytes 392 | tf_op jit(solution)/shard_map/while/body/eval_jaxpr/ppermute | solution.py:12
  44.3 1.6 %copy-start.1 = (bf16[1,4096,128]{2,1,0:T(8,128)(2,1)S(1)}, bf16[1,4096,128]{2,1,0:T(8,128)(2,1)}, u32[]{:S(2)}) copy-start(bf16[1,4096,128]{2,1,0:T(8,128)(2,1)} %get-tuple-element.197) | copy-start | bytes 3145732 | tf_op jit(solution)/shard_map/while
  47.6 7.5 %collective-permute-start.1 = (f32[8,4096]{1,0:T(8,128)S(1)}, f32[8,4096]{1,0:T(8,128)S(1)}, u32[]{:S(2)}, u32[]{:S(2)}) collective-permute-start(f32[8,4096]{1,0:T(8,128)S(1)} %fusion.53), channel_id=1, source_target_pairs={{24,0},{0,8},{8,16},{16,24},{25,1},{1,9},{9,17},{17,25},{26,2},{2,... | collective-permute-start | bytes 393224 | tf_op jit(solution)/shard_map/while/body/eval_jaxpr/ppermute | solution.py:12
  47.6 7.5 %collective-permute-start = (bf16[8,4096]{1,0:T(8,128)(2,1)S(1)}, bf16[8,4096]{1,0:T(8,128)(2,1)S(1)}, u32[]{:S(2)}, u32[]{:S(2)}) collective-permute-start(bf16[8,4096]{1,0:T(8,128)(2,1)S(1)} %copy.19), channel_id=1, source_target_pairs={{24,0},{0,8},{8,16},{16,24},{25,1},{1,9},{9,17},{17,25},{26,2},{2,... | collective-permute-start | bytes 196616 | tf_op jit(solution)/shard_map/while/body/eval_jaxpr/ppermute | solution.py:12
  47.9 7.2 %collective-permute-start.2 = (f32[8,4]{0,1:T(4,128)S(1)}, f32[8,4]{0,1:T(4,128)S(1)}, u32[]{:S(2)}, u32[]{:S(2)}) collective-permute-start(f32[8,4]{0,1:T(4,128)S(1)} %copy.21), channel_id=1, source_target_pairs={{24,0},{0,8},{8,16},{16,24},{25,1},{1,9},{9,17},{17,25},{26,2},{2,... | collective-permute-start | bytes 392 | tf_op jit(solution)/shard_map/while/body/eval_jaxpr/ppermute | solution.py:12
  55.1 1.6 %copy-start.2 = (bf16[1,4096,128]{2,1,0:T(8,128)(2,1)S(1)}, bf16[1,4096,128]{2,1,0:T(8,128)(2,1)}, u32[]{:S(2)}) copy-start(bf16[1,4096,128]{2,1,0:T(8,128)(2,1)} %get-tuple-element.202) | copy-start | bytes 3145732
  58.4 6.8 %collective-permute-start.3 = (f32[8,4096]{1,0:T(8,128)S(1)}, f32[8,4096]{1,0:T(8,128)S(1)}, u32[]{:S(2)}, u32[]{:S(2)}) collective-permute-start(f32[8,4096]{1,0:T(8,128)S(1)} %fusion.14), channel_id=1, source_target_pairs={{24,0},{0,8},{8,16},{16,24},{25,1},{1,9},{9,17},{17,25},{26,2},{2,... | collective-permute-start | bytes 393224 | tf_op jit(solution)/shard_map/ppermute | solution.py:12
  65.2 0.7 copy-start.4
  65.9 0.7 copy-start.7
Sparse Core Ops, SparseCore 0:
  66.0 50.1 all-reduce.2
where the time goes:
time: 126 us; the launch traced here: 125 us
  waiting for transfers between devices  72 us (57%)
  between operations  14.1 us (11%)
  matrix products  13.2 us (10%)
  blocking collectives  10.7 us (8%)
  starting transfers between devices  8.76 us (7%)
  other arithmetic  3.62 us (3%)
  local copies, waits for them, and re-layouts  2.68 us (2%)
    unnamed x2, waiting for transfers between devices  49.1 us
    ppermute x10, waiting for transfers between devices, shifted(): return lax.ppermute(block, axis, route)  23 us
    all_gather x1, blocking collectives, on_device(): row_block = lax.all_gather(normed, 'replica', axis=0, tiled=True)  10.7 us
    ppermute x10, starting transfers between devices, shifted(): return lax.ppermute(block, axis, route)  8.76 us
    dot_general x4, matrix products, expert_part(): return jnp.dot(hidden, down_slice, preferred_element_type=jnp.float32)  6.83 us
    dot_general x4, matrix products, expert_part(): gate_act = jnp.dot(normed, gate_slice, preferred_element_type=jnp.float32)  6.22 us
    unnamed x16, local copies, waits for them, and re-layouts  2.59 us
  transfers between devices with their start and end apart: 11, of which 5 were waited for; matrix products, arithmetic and copies ran while one was open for 0% of the time, Pallas kernels for 0%

commit v1 on v0

v1 whole, which is shorter than its diff:
```python
import functools

import jax
import jax.numpy as jnp
from jax import lax
from jax.experimental import pallas as pl
from jax.experimental.pallas import tpu as pltpu
from jax.sharding import PartitionSpec as P

ROUTE_SCALE = 2.5
LANES = 128


def moe_kernel(
    Z,
    R,
    x_ref,
    gain_ref,
    router_ref,
    routes_ref,
    gate_ref,
    up_ref,
    down_ref,
    out_ref,
    wgu,
    wd,
    xs,
    rows,
    flat,
    lhs,
    part,
    snd,
    got,
    acc,
    zsnd,
    zgot,
    wts,
    w_sem,
    ag_zsend,
    ag_zrecv,
    ag_psend,
    ag_precv,
    rs_psend,
    rs_precv,
    rs_zsend,
    rs_zrecv,
):
    C = xs.shape[0]
    F = wd.shape[0]
    M = Z * R
    z = lax.axis_index("expert")
    r = lax.axis_index("replica")
    z_peers = [(d, lax.rem(z + d, Z)) for d in range(1, Z)]
    r_peers = [(d, lax.rem(r + d, R)) for d in range(1, R)]

    barrier = pltpu.get_barrier_semaphore()
    for _, zp in z_peers:
        pl.semaphore_signal(
            barrier, inc=1, device_id={"expert": zp}, device_id_type=pl.DeviceIdType.MESH
        )
    for _, rp in r_peers:
        pl.semaphore_signal(
            barrier, inc=1, device_id={"replica": rp}, device_id_type=pl.DeviceIdType.MESH
        )

    weights = [
        pltpu.make_async_copy(gate_ref.at[0], wgu.at[:, pl.ds(0, F)], w_sem.at[0]),
        pltpu.make_async_copy(up_ref.at[0], wgu.at[:, pl.ds(F, F)], w_sem.at[1]),
        pltpu.make_async_copy(down_ref.at[0], wd, w_sem.at[2]),
    ]
    for copy in weights:
        copy.start()

    for c in range(C):
        xs[pl.ds(c, 1), :] = x_ref[:, pl.ds(c * LANES, LANES)].astype(jnp.float32)
    x = xs[...]
    squares = jnp.sum(jnp.sum(x * x, axis=0, keepdims=True), axis=1, keepdims=True)
    inverse_rms = lax.rsqrt(squares / (C * LANES) + 1e-06)
    normed = (x * inverse_rms * gain_ref[...]).astype(jnp.bfloat16)
    rows[r, z] = normed

    pl.semaphore_wait(barrier, (Z - 1) + (R - 1))

    def z_copy(d, zp, own):
        return pltpu.make_async_remote_copy(
            src_ref=rows.at[r, z],
            dst_ref=rows.at[r, z] if own else rows.at[r, zp],
            send_sem=ag_zsend.at[d],
            recv_sem=ag_zrecv.at[z] if own else ag_zrecv.at[zp],
            device_id={"expert": zp},
            device_id_type=pl.DeviceIdType.MESH,
        )

    def p_send(k, row_z, d, rp):
        return pltpu.make_async_remote_copy(
            src_ref=rows.at[r, row_z],
            dst_ref=rows.at[r, row_z],
            send_sem=ag_psend.at[k, d],
            recv_sem=ag_precv.at[row_z, r],
            device_id={"replica": rp},
            device_id_type=pl.DeviceIdType.MESH,
        )

    def p_recv(k, row_z, d, rp):
        return pltpu.make_async_remote_copy(
            src_ref=rows.at[rp, row_z],
            dst_ref=rows.at[rp, row_z],
            send_sem=ag_psend.at[k, d],
            recv_sem=ag_precv.at[row_z, rp],
            device_id={"replica": rp},
            device_id_type=pl.DeviceIdType.MESH,
        )

    for d, zp in z_peers:
        z_copy(d, zp, True).start()
    for d, rp in r_peers:
        p_send(0, z, d, rp).start()

    def spread(rr, zz):
        at = pl.multiple_of((rr * Z + zz) * C, C)
        flat[pl.ds(at, C), :] = rows[rr, zz].astype(jnp.float32)

    for d, zp in z_peers:
        z_copy(d, zp, False).wait_recv()
        for e, rp in r_peers:
            p_send(d, zp, e, rp).start()

    E = router_ref.shape[0]
    xs[...] = normed.astype(jnp.float32)
    logit_sums = jnp.zeros((E, LANES), jnp.float32)
    for c in range(C):
        logit_sums += (
            router_ref[:, pl.ds(c * LANES, LANES)].astype(jnp.float32) * xs[pl.ds(c, 1), :]
        )
    logits = jnp.broadcast_to(jnp.sum(logit_sums, axis=1, keepdims=True), (E, LANES))
    expert_ids = lax.broadcasted_iota(jnp.int32, (E, LANES), 0)
    members = jnp.zeros((E, LANES), jnp.float32)
    for t in range(routes_ref.shape[0]):
        members += (expert_ids == routes_ref[t, r]).astype(jnp.float32)
    chosen = members / (1.0 + jnp.exp(-logits))
    wts[...] = ROUTE_SCALE * chosen / jnp.sum(chosen, axis=0, keepdims=True)

    spread(r, z)
    for _, zp in z_peers:
        spread(r, zp)
    for k, zz in [(0, z)] + z_peers:
        for e, rp in r_peers:
            p_recv(k, zz, e, rp).wait_recv()
            spread(rp, zz)
    for c in range(C):
        lhs[:, pl.ds(c * LANES, LANES)] = flat[pl.ds(c, M, stride=C), :].astype(jnp.bfloat16)

    weights[0].wait()
    weights[1].wait()
    gate_up = jnp.dot(lhs[...], wgu[...], preferred_element_type=jnp.float32)
    gate_act, up_act = gate_up[:, :F], gate_up[:, F:]
    hidden = (gate_act / (1.0 + jnp.exp(-gate_act)) * up_act).astype(jnp.bfloat16)
    weights[2].wait()
    step = 4
    for n in range(C // step):
        piece = jnp.dot(
            hidden,
            wd[:, pl.ds(n * step * LANES, step * LANES)],
            preferred_element_type=jnp.float32,
        )
        for j in range(step):
            part[pl.ds(n * step + j, M, stride=C), :] = piece[:, j * LANES : (j + 1) * LANES]

    span = Z * C

    def rs_send(d, rp):
        return pltpu.make_async_remote_copy(
            src_ref=snd.at[rp],
            dst_ref=got.at[r],
            send_sem=rs_psend.at[d],
            recv_sem=rs_precv.at[r],
            device_id={"replica": rp},
            device_id_type=pl.DeviceIdType.MESH,
        )

    def rs_recv(d, rp):
        return pltpu.make_async_remote_copy(
            src_ref=snd.at[rp],
            dst_ref=got.at[rp],
            send_sem=rs_psend.at[d],
            recv_sem=rs_precv.at[rp],
            device_id={"replica": rp},
            device_id_type=pl.DeviceIdType.MESH,
        )

    for d, rp in r_peers:
        at = pl.multiple_of(rp * span, span)
        snd[rp] = part[pl.ds(at, span), :].astype(jnp.bfloat16)
        rs_send(d, rp).start()
    acc[...] = part[pl.ds(pl.multiple_of(r * span, span), span), :]
    for d, rp in r_peers:
        rs_recv(d, rp).wait_recv()
        acc[...] += got[rp].astype(jnp.float32)

    def rz_copy(d, zp, own):
        return pltpu.make_async_remote_copy(
            src_ref=zsnd.at[zp],
            dst_ref=zgot.at[z] if own else zgot.at[zp],
            send_sem=rs_zsend.at[d],
            recv_sem=rs_zrecv.at[z] if own else rs_zrecv.at[zp],
            device_id={"expert": zp},
            device_id_type=pl.DeviceIdType.MESH,
        )

    for d, zp in z_peers:
        zsnd[zp] = acc[pl.ds(pl.multiple_of(zp * C, C), C), :].astype(jnp.bfloat16)
        rz_copy(d, zp, True).start()
    total = acc[pl.ds(pl.multiple_of(z * C, C), C), :] * wts[pl.ds(z, 1), :]
    for d, zp in z_peers:
        rz_copy(d, zp, False).wait_recv()
        total += zgot[zp].astype(jnp.float32) * wts[pl.ds(zp, 1), :]

    for c in range(C):
        lane = pl.ds(c * LANES, LANES)
        out_ref[:, lane] = (
            x_ref[:, lane].astype(jnp.float32) + total[c : c + 1, :]
        ).astype(jnp.bfloat16)

    for d, zp in z_peers:
        z_copy(d, zp, True).wait_send()
        rz_copy(d, zp, True).wait_send()
        for e, rp in r_peers:
            p_send(d, zp, e, rp).wait_send()
    for d, rp in r_peers:
        p_send(0, z, d, rp).wait_send()
        rs_send(d, rp).wait_send()


def solution(mesh):
    Z, R = mesh.shape["expert"], mesh.shape["replica"]

    def on_device(beam_rows, norm_gain, router, gate_proj, up_proj, down_proj, routes):
        D = beam_rows.shape[1]
        F = gate_proj.shape[2]
        C = D // LANES
        M = Z * R
        E = router.shape[1]
        vmem = pl.BlockSpec(memory_space=pltpu.VMEM)
        smem = pl.BlockSpec(memory_space=pltpu.SMEM)
        anywhere = pl.BlockSpec(memory_space=pl.ANY)
        dma = pltpu.SemaphoreType.DMA
        return pl.pallas_call(
            functools.partial(moe_kernel, Z, R),
            out_shape=jax.ShapeDtypeStruct(beam_rows.shape, jnp.bfloat16),
            in_specs=[vmem, vmem, vmem, smem, anywhere, anywhere, anywhere],
            out_specs=vmem,
            scratch_shapes=[
                pltpu.VMEM((D, 2 * F), jnp.bfloat16),
                pltpu.VMEM((F, D), jnp.bfloat16),
                pltpu.VMEM((C, LANES), jnp.float32),
                pltpu.VMEM((R, Z, C, LANES), jnp.bfloat16),
                pltpu.VMEM((M * C, LANES), jnp.float32),
                pltpu.VMEM((M, D), jnp.bfloat16),
                pltpu.VMEM((M * C, LANES), jnp.float32),
                pltpu.VMEM((R, Z * C, LANES), jnp.bfloat16),
                pltpu.VMEM((R, Z * C, LANES), jnp.bfloat16),
                pltpu.VMEM((Z * C, LANES), jnp.float32),
                pltpu.VMEM((Z, C, LANES), jnp.bfloat16),
                pltpu.VMEM((Z, C, LANES), jnp.bfloat16),
                pltpu.VMEM((E, LANES), jnp.float32),
                dma((3,)),
                dma((Z,)),
                dma((Z,)),
                dma((Z, R)),
                dma((Z, R)),
                dma((R,)),
                dma((R,)),
                dma((Z,)),
                dma((Z,)),
            ],
            compiler_params=pltpu.CompilerParams(
                collective_id=0, has_side_effects=True, vmem_limit_bytes=50 * 2**20
            ),
        )(
            beam_rows,
            norm_gain.reshape(C, LANES),
            router.T,
            routes.T,
            gate_proj,
            up_proj,
            down_proj,
        )

    placed = (
        P(("groups", "expert", "replica"), None),
        P(),
        P(),
        P("expert", None, "replica"),
        P("expert", None, "replica"),
        P("expert", "replica", None),
        P(("groups", "expert"), None),
    )
    return jax.shard_map(
        on_device,
        mesh=mesh,
        in_specs=placed,
        out_specs=P(("groups", "expert", "replica"), None),
        check_vma=False,
    )
```

time: 126 us -> 31.8 us (0.25)
  waiting for transfers between devices: 72 us -> 0 us
  Pallas kernels: 0 us -> 24.2 us
  between operations: 14.1 us -> 0.02 us
  matrix products: 13.2 us -> 0 us
  blocking collectives: 10.7 us -> 0 us
  starting transfers between devices: 8.76 us -> 0 us
  local copies, waits for them, and re-layouts: 2.68 us -> 7.15 us
  other arithmetic: 3.62 us -> 0 us
    unnamed x2 -> x0, waiting for transfers between devices: 49.1 us -> none
    pallas_call x0 -> x1, Pallas kernels: none -> 24.2 us  [on_device(): pl.pallas_call(functools.partial(moe_kernel, Z, R), out_shape=jax.ShapeDt...]
    ppermute x10 -> x0, waiting for transfers between devices: 23 us -> none  [shifted(): return lax.ppermute(block, axis, route)]
    dot_general x9 -> x0, matrix products: 13.2 us -> none  [the longest x4 6.83 us: expert_part(): return jnp.dot(hidden, down_slice, preferred_element_type=jnp.float32)]
    all_gather x1 -> x0, blocking collectives: 10.7 us -> none  [on_device(): row_block = lax.all_gather(normed, 'replica', axis=0, tiled=True)]
    ppermute x10 -> x0, starting transfers between devices: 8.76 us -> none  [shifted(): return lax.ppermute(block, axis, route)]
    unnamed x16 -> x15, local copies, waits for them, and re-layouts: 2.59 us -> 7.15 us
    convert_element_type x1 -> x0, other arithmetic: 2.16 us -> none  [on_device(): return (beam_rows.astype(jnp.float32) + row_share).astype(jnp.bfloat16)]
  transfers between devices with their start and end apart: 11 -> 0, of which waited for: 5 -> 0; matrix products, arithmetic and copies ran while one was open for 0% -> 0% of each run, Pallas kernels for 0% -> 0%
where the time goes in v1:
time: 31.8 us; the launch traced here: 31.4 us
  Pallas kernels  24.2 us (76%)
  local copies, waits for them, and re-layouts  7.15 us (22%)
    pallas_call x1, Pallas kernels, on_device(): pl.pallas_call(functools.partial(moe_kernel, Z, R), out_shape=jax.ShapeDt...  24.2 us
    unnamed x15, local copies, waits for them, and re-layouts  7.15 us

profile of v1, /device:TPU:0, one launch (start us, length us, event | category | flops | bytes accessed | tf_op | source)
XLA Modules:
  0.0 31.4 jit_solution(10241942505947801798)
XLA Ops:
  0.0 0.0 copy-start.6
  0.0 0.7 %copy-done.6 = s32[8,2]{0,1:T(2,128)S(1)} copy-done((s32[8,2]{0,1:T(2,128)S(1)}, s32[8,2]{0,1:T(2,128)}, u32[]{:S(2)}) %copy-start.6) | copy-done | bytes 88
  0.7 0.0 copy-start
  0.7 1.2 %copy-done = bf16[1,4096,128]{2,1,0:T(8,128)(2,1)S(1)} copy-done((bf16[1,4096,128]{2,1,0:T(8,128)(2,1)S(1)}, bf16[1,4096,128]{2,1,0:T(8,128)(2,1)}, u32[]{:S(2)}) %copy-start) | copy-done | bytes 1048600
  1.9 0.0 copy-start.1
  1.9 1.2 %copy-done.1 = bf16[1,4096,128]{2,1,0:T(8,128)(2,1)S(1)} copy-done((bf16[1,4096,128]{2,1,0:T(8,128)(2,1)S(1)}, bf16[1,4096,128]{2,1,0:T(8,128)(2,1)}, u32[]{:S(2)}) %copy-start.1) | copy-done | bytes 1048600
  3.1 0.0 copy-start.2
  3.1 1.2 %copy-done.2 = bf16[1,128,4096]{2,1,0:T(8,128)(2,1)S(1)} copy-done((bf16[1,128,4096]{2,1,0:T(8,128)(2,1)S(1)}, bf16[1,128,4096]{2,1,0:T(8,128)(2,1)}, u32[]{:S(2)}) %copy-start.2) | copy-done | bytes 1048600
  4.4 0.0 copy-start.3
  4.4 0.8 %copy-done.3 = bf16[4096,4]{0,1:T(4,128)(2,1)S(1)} copy-done((bf16[4096,4]{0,1:T(4,128)(2,1)S(1)}, bf16[4096,4]{0,1:T(4,128)(2,1)}, u32[]{:S(2)}) %copy-start.3) | copy-done | bytes 32792
  5.1 0.0 copy-start.4
  5.1 0.7 %copy-done.4 = bf16[1,4096]{1,0:T(2,128)(2,1)S(1)} copy-done((bf16[1,4096]{1,0:T(2,128)(2,1)S(1)}, bf16[1,4096]{1,0:T(2,128)(2,1)}, u32[]{:S(2)}) %copy-start.4) | copy-done | bytes 8216
  5.8 0.0 copy-start.5
  5.8 0.7 %copy-done.5 = f32[4096]{0:T(1024)S(1)} copy-done((f32[4096]{0:T(1024)S(1)}, f32[4096]{0:T(1024)}, u32[]{:S(2)}) %copy-start.5) | copy-done | bytes 16408
  6.5 24.2 %shard_map.73 = bf16[1,4096]{1,0:T(2,128)(2,1)S(1)} custom-call(bf16[1,4096]{1,0:T(2,128)(2,1)S(1)} %copy-done.4, f32[32,128]{1,0:T(8,128)S(1)} %bitcast.4, bf16[4,4096]{1,0:T(4,128)(2,1)S(1)} %bitcast.3, s32[2,8]{1,0:T(2,128)S(1)} %bitcast.5, bf16[1,4096,128]{2,1,0:T(8,128)(2,1)S(1)} %copy-done, bf16[1,4096,128]{2,1,0:T(8,128)(2,1)S(1)} %copy-done.1, ...), custom_call_target="tpu_custom_call" | custom-call | tf_op jit(solution)/shard_map/pallas_call | solution.py:247
  30.8 0.6 %copy.9 = bf16[1,4096]{1,0:T(2,128)(2,1)} copy(bf16[1,4096]{1,0:T(2,128)(2,1)S(1)} %shard_map.73) | data formatting | bytes 16384
Async XLA Ops:
  0.0 0.7 %copy-start.6 = (s32[8,2]{0,1:T(2,128)S(1)}, s32[8,2]{0,1:T(2,128)}, u32[]{:S(2)}) copy-start(s32[8,2]{0,1:T(2,128)} %param.13) | copy-start | bytes 196
  0.7 1.2 %copy-start = (bf16[1,4096,128]{2,1,0:T(8,128)(2,1)S(1)}, bf16[1,4096,128]{2,1,0:T(8,128)(2,1)}, u32[]{:S(2)}) copy-start(bf16[1,4096,128]{2,1,0:T(8,128)(2,1)} %gate_ref.1) | copy-start | bytes 3145732
  1.9 1.2 %copy-start.1 = (bf16[1,4096,128]{2,1,0:T(8,128)(2,1)S(1)}, bf16[1,4096,128]{2,1,0:T(8,128)(2,1)}, u32[]{:S(2)}) copy-start(bf16[1,4096,128]{2,1,0:T(8,128)(2,1)} %up_ref.1) | copy-start | bytes 3145732
  3.1 1.2 %copy-start.2 = (bf16[1,128,4096]{2,1,0:T(8,128)(2,1)S(1)}, bf16[1,128,4096]{2,1,0:T(8,128)(2,1)}, u32[]{:S(2)}) copy-start(bf16[1,128,4096]{2,1,0:T(8,128)(2,1)} %down_ref.1) | copy-start | bytes 3145732
  4.4 0.8 %copy-start.3 = (bf16[4096,4]{0,1:T(4,128)(2,1)S(1)}, bf16[4096,4]{0,1:T(4,128)(2,1)}, u32[]{:S(2)}) copy-start(bf16[4096,4]{0,1:T(4,128)(2,1)} %param.9) | copy-start | bytes 98308
  5.1 0.7 %copy-start.4 = (bf16[1,4096]{1,0:T(2,128)(2,1)S(1)}, bf16[1,4096]{1,0:T(2,128)(2,1)}, u32[]{:S(2)}) copy-start(bf16[1,4096]{1,0:T(2,128)(2,1)} %x_ref.1) | copy-start | bytes 24580
  5.8 0.7 %copy-start.5 = (f32[4096]{0:T(1024)S(1)}, f32[4096]{0:T(1024)}, u32[]{:S(2)}) copy-start(f32[4096]{0:T(1024)} %param.8) | copy-start | bytes 49156

commit v2 on v1

--- a/solution.py
+++ b/solution.py
@@ -9,19 +9,24 @@
 
 ROUTE_SCALE = 2.5
 LANES = 128
+VMEM_BYTES = 63 * 2**20
 
 
 def moe_kernel(
     Z,
     R,
+    x_hbm,
+    gain_hbm,
+    router_hbm,
+    routes_hbm,
+    gate_ref,
+    up_ref,
+    down_ref,
+    out_ref,
     x_ref,
     gain_ref,
     router_ref,
     routes_ref,
-    gate_ref,
-    up_ref,
-    down_ref,
-    out_ref,
     wgu,
     wd,
     xs,
@@ -53,6 +58,15 @@
     z_peers = [(d, lax.rem(z + d, Z)) for d in range(1, Z)]
     r_peers = [(d, lax.rem(r + d, R)) for d in range(1, R)]
 
+    small = [
+        pltpu.make_async_copy(x_hbm, x_ref, w_sem.at[3]),
+        pltpu.make_async_copy(gain_hbm, gain_ref, w_sem.at[4]),
+        pltpu.make_async_copy(router_hbm, router_ref, w_sem.at[5]),
+        pltpu.make_async_copy(routes_hbm, routes_ref, w_sem.at[6]),
+    ]
+    for copy in small:
+        copy.start()
+
     barrier = pltpu.get_barrier_semaphore()
     for _, zp in z_peers:
         pl.semaphore_signal(
@@ -71,6 +85,8 @@
     for copy in weights:
         copy.start()
 
+    small[0].wait()
+    small[1].wait()
     for c in range(C):
         xs[pl.ds(c, 1), :] = x_ref[:, pl.ds(c * LANES, LANES)].astype(jnp.float32)
     x = xs[...]
@@ -125,6 +141,8 @@
         for e, rp in r_peers:
             p_send(d, zp, e, rp).start()
 
+    small[2].wait()
+    small[3].wait()
     E = router_ref.shape[0]
     xs[...] = normed.astype(jnp.float32)
     logit_sums = jnp.zeros((E, LANES), jnp.float32)
@@ -241,15 +259,18 @@
         M = Z * R
         E = router.shape[1]
         vmem = pl.BlockSpec(memory_space=pltpu.VMEM)
-        smem = pl.BlockSpec(memory_space=pltpu.SMEM)
         anywhere = pl.BlockSpec(memory_space=pl.ANY)
         dma = pltpu.SemaphoreType.DMA
         return pl.pallas_call(
             functools.partial(moe_kernel, Z, R),
             out_shape=jax.ShapeDtypeStruct(beam_rows.shape, jnp.bfloat16),
-            in_specs=[vmem, vmem, vmem, smem, anywhere, anywhere, anywhere],
+            in_specs=[anywhere] * 7,
             out_specs=vmem,
             scratch_shapes=[
+                pltpu.VMEM(beam_rows.shape, beam_rows.dtype),
+                pltpu.VMEM((C, LANES), jnp.float32),
+                pltpu.VMEM((E, D), router.dtype),
+                pltpu.SMEM(routes.shape[::-1], jnp.int32),
                 pltpu.VMEM((D, 2 * F), jnp.bfloat16),
                 pltpu.VMEM((F, D), jnp.bfloat16),
                 pltpu.VMEM((C, LANES), jnp.float32),
@@ -263,7 +284,7 @@
                 pltpu.VMEM((Z, C, LANES), jnp.bfloat16),
                 pltpu.VMEM((Z, C, LANES), jnp.bfloat16),
                 pltpu.VMEM((E, LANES), jnp.float32),
-                dma((3,)),
+                dma((7,)),
                 dma((Z,)),
                 dma((Z,)),
                 dma((Z, R)),
@@ -274,7 +295,7 @@
                 dma((Z,)),
             ],
             compiler_params=pltpu.CompilerParams(
-                collective_id=0, has_side_effects=True, vmem_limit_bytes=50 * 2**20
+                collective_id=0, has_side_effects=True, vmem_limit_bytes=VMEM_BYTES
             ),
         )(
             beam_rows,

time: 31.8 us -> 26 us (0.82)
  local copies, waits for them, and re-layouts: 7.15 us -> 1.34 us
    unnamed x15 -> x1, local copies, waits for them, and re-layouts: 7.15 us -> 1.34 us
where the time goes in v2:
time: 26 us; the launch traced here: 25.6 us
  Pallas kernels  24.3 us (93%)
  local copies, waits for them, and re-layouts  1.34 us (5%)
    pallas_call x1, Pallas kernels, on_device(): pl.pallas_call(functools.partial(moe_kernel, Z, R), out_shape=jax.ShapeDt...  24.3 us
    unnamed x1, local copies, waits for them, and re-layouts  1.34 us

profile of v2, /device:TPU:0, one launch (start us, length us, event | category | flops | bytes accessed | tf_op | source)
XLA Modules:
  0.0 25.6 jit_solution(6479632809177851514)
XLA Ops:
  0.0 24.3 %shard_map.73 = bf16[1,4096]{1,0:T(2,128)(2,1)} custom-call(bf16[1,4096]{1,0:T(2,128)(2,1)} %x_hbm.1, f32[32,128]{1,0:T(8,128)} %bitcast.4, bf16[4,4096]{1,0:T(4,128)(2,1)} %bitcast.3, s32[2,8]{1,0:T(2,128)} %bitcast.5, bf16[1,4096,128]{2,1,0:T(8,128)(2,1)} %gate_ref.1, bf16[1,4096,128]{2,1,0:T(8,128)(2,1)} %up_ref.1, bf16[1,128,4096]{2,1,0:T(8,128)(2,1)} %down_ref.1), custom_call_target="tpu_custom_call" | custom-call | tf_op jit(solution)/shard_map/pallas_call | solution.py:264
  24.3 1.3 %copy.9 = bf16[1,4096]{1,0:T(2,128)(2,1)} copy(bf16[1,4096]{1,0:T(2,128)(2,1)} %shard_map.73) | data formatting | bytes 16384

commit v3 on v2

v3 whole, which is shorter than its diff:
```python
import functools

import jax
import jax.numpy as jnp
from jax import lax
from jax.experimental import pallas as pl
from jax.experimental.pallas import tpu as pltpu
from jax.sharding import PartitionSpec as P

ROUTE_SCALE = 2.5
LANES = 128
VMEM_BYTES = 63 * 2**20


def moe_kernel(
    Z,
    R,
    x_hbm,
    gain_hbm,
    router_hbm,
    routes_hbm,
    gate_ref,
    up_ref,
    down_ref,
    out_ref,
    x_ref,
    gain_ref,
    router_ref,
    routes_ref,
    wgu,
    wd,
    xs,
    rows,
    flat,
    lhs,
    part,
    psnd,
    pgot,
    acc,
    snd,
    got,
    wts,
    w_sem,
    ag_send,
    ag_pass,
    ag_recv,
    rs_psend,
    rs_precv,
    rs_send,
    rs_recv,
):
    C = xs.shape[0]
    F = wd.shape[0]
    M = Z * R
    z = lax.axis_index("expert")
    r = lax.axis_index("replica")
    core = lax.rem(r, 2)
    partner = r + 1 - 2 * core
    MESH = pl.DeviceIdType.MESH

    def flip(value, mask):
        bit = 1
        while bit <= mask:
            if mask & bit:
                value = value + bit - 2 * bit * lax.rem(lax.div(value, bit), 2)
            bit *= 2
        return value

    pairs = [(a, 2 * b) for a in range(Z) for b in range(R // 2) if a or b]
    pairs.sort(key=lambda p: p[0] + bin(p[1]).count("1"))
    peers = [(i, flip(z, a), flip(r, b)) for i, (a, b) in enumerate(pairs)]

    small = [
        pltpu.make_async_copy(x_hbm, x_ref, w_sem.at[3]),
        pltpu.make_async_copy(gain_hbm, gain_ref, w_sem.at[4]),
        pltpu.make_async_copy(router_hbm, router_ref, w_sem.at[5]),
        pltpu.make_async_copy(routes_hbm, routes_ref, w_sem.at[6]),
    ]
    for copy in small:
        copy.start()

    barrier = pltpu.get_barrier_semaphore()
    pl.semaphore_signal(barrier, inc=1, device_id={"replica": partner}, device_id_type=MESH)
    for _, zp, rp in peers:
        pl.semaphore_signal(
            barrier, inc=1, device_id={"expert": zp, "replica": rp}, device_id_type=MESH
        )

    weights = [
        pltpu.make_async_copy(gate_ref.at[0], wgu.at[:, pl.ds(0, F)], w_sem.at[0]),
        pltpu.make_async_copy(up_ref.at[0], wgu.at[:, pl.ds(F, F)], w_sem.at[1]),
        pltpu.make_async_copy(down_ref.at[0], wd, w_sem.at[2]),
    ]
    for copy in weights:
        copy.start()

    small[0].wait()
    small[1].wait()
    for c in range(C):
        xs[pl.ds(c, 1), :] = x_ref[:, pl.ds(c * LANES, LANES)].astype(jnp.float32)
    x = xs[...]
    squares = jnp.sum(jnp.sum(x * x, axis=0, keepdims=True), axis=1, keepdims=True)
    inverse_rms = lax.rsqrt(squares / (C * LANES) + 1e-06)
    normed = (x * inverse_rms * gain_ref[...]).astype(jnp.bfloat16)
    rows[r, z] = normed

    pl.semaphore_wait(barrier, len(peers) + 1)

    def row_copy(rr, zz, send_sem, zp, rp):
        return pltpu.make_async_remote_copy(
            src_ref=rows.at[rr, zz],
            dst_ref=rows.at[rr, zz],
            send_sem=send_sem,
            recv_sem=ag_recv.at[rr, zz],
            device_id={"expert": zp, "replica": rp},
            device_id_type=MESH,
        )

    for i, zp, rp in reversed(peers):
        row_copy(r, z, ag_send.at[i], zp, rp).start()
    row_copy(r, z, ag_send.at[len(peers)], z, partner).start()

    def spread(rr, zz):
        at = pl.multiple_of((rr * Z + zz) * C, C)
        flat[pl.ds(at, C), :] = rows[rr, zz].astype(jnp.float32)

    small[2].wait()
    small[3].wait()
    E = router_ref.shape[0]
    xs[...] = normed.astype(jnp.float32)
    logit_sums = jnp.zeros((E, LANES), jnp.float32)
    for c in range(C):
        logit_sums += (
            router_ref[:, pl.ds(c * LANES, LANES)].astype(jnp.float32) * xs[pl.ds(c, 1), :]
        )
    logits = jnp.broadcast_to(jnp.sum(logit_sums, axis=1, keepdims=True), (E, LANES))
    expert_ids = lax.broadcasted_iota(jnp.int32, (E, LANES), 0)
    members = jnp.zeros((E, LANES), jnp.float32)
    for t in range(routes_ref.shape[0]):
        members += (expert_ids == routes_ref[t, r]).astype(jnp.float32)
    chosen = members / (1.0 + jnp.exp(-logits))
    wts[...] = ROUTE_SCALE * chosen / jnp.sum(chosen, axis=0, keepdims=True)

    spread(r, z)
    for i, zp, rp in peers:
        row_copy(rp, zp, ag_send.at[i], zp, rp).wait_recv()
        row_copy(rp, zp, ag_pass.at[i], z, partner).start()
        spread(rp, zp)
    for i, zp, rp in [(len(peers), z, r)] + peers:
        other = rp + partner - r
        row_copy(other, zp, ag_send.at[i], z, partner).wait_recv()
        spread(other, zp)
    for c in range(C):
        lhs[:, pl.ds(c * LANES, LANES)] = flat[pl.ds(c, M, stride=C), :].astype(jnp.bfloat16)

    weights[0].wait()
    weights[1].wait()
    gate_up = jnp.dot(lhs[...], wgu[...], preferred_element_type=jnp.float32)
    gate_act, up_act = gate_up[:, :F], gate_up[:, F:]
    hidden = (gate_act / (1.0 + jnp.exp(-gate_act)) * up_act).astype(jnp.bfloat16)
    weights[2].wait()
    step = 4
    for n in range(C // step):
        piece = jnp.dot(
            hidden,
            wd[:, pl.ds(n * step * LANES, step * LANES)],
            preferred_element_type=jnp.float32,
        )
        for j in range(step):
            part[pl.ds(n * step + j, M, stride=C), :] = piece[:, j * LANES : (j + 1) * LANES]

    span = Z * C
    half = R // 2

    def pair_copy(k):
        return pltpu.make_async_remote_copy(
            src_ref=psnd.at[k],
            dst_ref=pgot.at[k],
            send_sem=rs_psend.at[k],
            recv_sem=rs_precv.at[k],
            device_id={"replica": partner},
            device_id_type=MESH,
        )

    mine_k = lax.div(r, 2)
    order = [lax.div(flip(r, 2 * b), 2) for b in reversed(range(half))]
    for k in order:
        at = pl.multiple_of((2 * k + 1 - core) * span, span)
        psnd[k] = part[pl.ds(at, span), :].astype(jnp.bfloat16)
        pair_copy(k).start()

    def sum_copy(i, zp, rp, own):
        kp = lax.div(rp, 2)
        slot = (mine_k, z) if own else (kp, zp)
        return pltpu.make_async_remote_copy(
            src_ref=snd.at[kp, zp],
            dst_ref=got.at[slot[0], slot[1]],
            send_sem=rs_send.at[i],
            recv_sem=rs_recv.at[slot[0], slot[1]],
            device_id={"expert": zp, "replica": rp},
            device_id_type=MESH,
        )

    for b in reversed(range(half)):
        k = order[half - 1 - b]
        pair_copy(k).wait_recv()
        at = pl.multiple_of((2 * k + core) * span, span)
        acc[...] = part[pl.ds(at, span), :] + pgot[k].astype(jnp.float32)
        for (i, zp, rp), (_, bb) in reversed(list(zip(peers, pairs))):
            if bb == 2 * b:
                snd[k, zp] = acc[pl.ds(pl.multiple_of(zp * C, C), C), :].astype(jnp.bfloat16)
                sum_copy(i, zp, rp, True).start()
    total = acc[pl.ds(pl.multiple_of(z * C, C), C), :] * wts[pl.ds(z, 1), :]
    for i, zp, rp in peers:
        sum_copy(i, zp, rp, False).wait_recv()
        total += got[lax.div(rp, 2), zp].astype(jnp.float32) * wts[pl.ds(zp, 1), :]

    for c in range(C):
        lane = pl.ds(c * LANES, LANES)
        out_ref[:, lane] = (
            x_ref[:, lane].astype(jnp.float32) + total[c : c + 1, :]
        ).astype(jnp.bfloat16)

    for i, zp, rp in peers:
        row_copy(r, z, ag_send.at[i], zp, rp).wait_send()
        row_copy(rp, zp, ag_pass.at[i], z, partner).wait_send()
        sum_copy(i, zp, rp, True).wait_send()
    row_copy(r, z, ag_send.at[len(peers)], z, partner).wait_send()
    for k in order:
        pair_copy(k).wait_send()


def solution(mesh):
    Z, R = mesh.shape["expert"], mesh.shape["replica"]

    def on_device(beam_rows, norm_gain, router, gate_proj, up_proj, down_proj, routes):
        D = beam_rows.shape[1]
        F = gate_proj.shape[2]
        C = D // LANES
        M = Z * R
        E = router.shape[1]
        vmem = pl.BlockSpec(memory_space=pltpu.VMEM)
        anywhere = pl.BlockSpec(memory_space=pl.ANY)
        dma = pltpu.SemaphoreType.DMA
        return pl.pallas_call(
            functools.partial(moe_kernel, Z, R),
            out_shape=jax.ShapeDtypeStruct(beam_rows.shape, jnp.bfloat16),
            in_specs=[anywhere] * 7,
            out_specs=vmem,
            scratch_shapes=[
                pltpu.VMEM(beam_rows.shape, beam_rows.dtype),
                pltpu.VMEM((C, LANES), jnp.float32),
                pltpu.VMEM((E, D), router.dtype),
                pltpu.SMEM(routes.shape[::-1], jnp.int32),
                pltpu.VMEM((D, 2 * F), jnp.bfloat16),
                pltpu.VMEM((F, D), jnp.bfloat16),
                pltpu.VMEM((C, LANES), jnp.float32),
                pltpu.VMEM((R, Z, C, LANES), jnp.bfloat16),
                pltpu.VMEM((M * C, LANES), jnp.float32),
                pltpu.VMEM((M, D), jnp.bfloat16),
                pltpu.VMEM((M * C, LANES), jnp.float32),
                pltpu.VMEM((R // 2, Z * C, LANES), jnp.bfloat16),
                pltpu.VMEM((R // 2, Z * C, LANES), jnp.bfloat16),
                pltpu.VMEM((Z * C, LANES), jnp.float32),
                pltpu.VMEM((R // 2, Z, C, LANES), jnp.bfloat16),
                pltpu.VMEM((R // 2, Z, C, LANES), jnp.bfloat16),
                pltpu.VMEM((E, LANES), jnp.float32),
                dma((7,)),
                dma((M // 2,)),
                dma((M // 2,)),
                dma((R, Z)),
                dma((R // 2,)),
                dma((R // 2,)),
                dma((M // 2,)),
                dma((R // 2, Z)),
            ],
            compiler_params=pltpu.CompilerParams(
                collective_id=0, has_side_effects=True, vmem_limit_bytes=VMEM_BYTES
            ),
        )(
            beam_rows,
            norm_gain.reshape(C, LANES),
            router.T,
            routes.T,
            gate_proj,
            up_proj,
            down_proj,
        )

    placed = (
        P(("groups", "expert", "replica"), None),
        P(),
        P(),
        P("expert", None, "replica"),
        P("expert", None, "replica"),
        P("expert", "replica", None),
        P(("groups", "expert"), None),
    )
    return jax.shard_map(
        on_device,
        mesh=mesh,
        in_specs=placed,
        out_specs=P(("groups", "expert", "replica"), None),
        check_vma=False,
    )
```

time: 26 us -> 23 us (0.88)
  Pallas kernels: 24.3 us -> 21.3 us
    pallas_call x1, Pallas kernels: 24.3 us -> 21.3 us  [on_device(): pl.pallas_call(functools.partial(moe_kernel, Z, R), out_shape=jax.ShapeDt...]
where the time goes in v3:
time: 23 us; the launch traced here: 22.7 us
  Pallas kernels  21.3 us (93%)
  local copies, waits for them, and re-layouts  1.34 us (6%)
    pallas_call x1, Pallas kernels, on_device(): pl.pallas_call(functools.partial(moe_kernel, Z, R), out_shape=jax.ShapeDt...  21.3 us
    unnamed x1, local copies, waits for them, and re-layouts  1.34 us

profile of v3, /device:TPU:0, one launch (start us, length us, event | category | flops | bytes accessed | tf_op | source)
XLA Modules:
  0.0 22.7 jit_solution(8210741384935676148)
XLA Ops:
  0.0 21.3 %shard_map.73 = bf16[1,4096]{1,0:T(2,128)(2,1)} custom-call(bf16[1,4096]{1,0:T(2,128)(2,1)} %x_hbm.1, f32[32,128]{1,0:T(8,128)} %bitcast.4, bf16[4,4096]{1,0:T(4,128)(2,1)} %bitcast.3, s32[2,8]{1,0:T(2,128)} %bitcast.5, bf16[1,4096,128]{2,1,0:T(8,128)(2,1)} %gate_ref.1, bf16[1,4096,128]{2,1,0:T(8,128)(2,1)} %up_ref.1, bf16[1,128,4096]{2,1,0:T(8,128)(2,1)} %down_ref.1), custom_call_target="tpu_custom_call" | custom-call | tf_op jit(solution)/shard_map/pallas_call | solution.py:245
  21.3 1.3 %copy.9 = bf16[1,4096]{1,0:T(2,128)(2,1)} copy(bf16[1,4096]{1,0:T(2,128)(2,1)} %shard_map.73) | data formatting | bytes 16384

commit v4 on v3

--- a/solution.py
+++ b/solution.py
@@ -34,28 +34,26 @@
     flat,
     lhs,
     part,
-    psnd,
-    pgot,
-    acc,
     snd,
     got,
     wts,
     w_sem,
     ag_send,
-    ag_pass,
     ag_recv,
-    rs_psend,
-    rs_precv,
+    share_send,
+    share_recv,
     rs_send,
     rs_recv,
 ):
     C = xs.shape[0]
-    F = wd.shape[0]
-    M = Z * R
+    F = down_ref.shape[1]
+    half = R // 2
+    M = Z * half
     z = lax.axis_index("expert")
     r = lax.axis_index("replica")
     core = lax.rem(r, 2)
     partner = r + 1 - 2 * core
+    mine = lax.div(r, 2)
     MESH = pl.DeviceIdType.MESH
 
     def flip(value, mask):
@@ -89,7 +87,7 @@
     weights = [
         pltpu.make_async_copy(gate_ref.at[0], wgu.at[:, pl.ds(0, F)], w_sem.at[0]),
         pltpu.make_async_copy(up_ref.at[0], wgu.at[:, pl.ds(F, F)], w_sem.at[1]),
-        pltpu.make_async_copy(down_ref.at[0], wd, w_sem.at[2]),
+        pltpu.make_async_copy(down_ref.at[0], wd.at[pl.ds(0, F), :], w_sem.at[2]),
     ]
     for copy in weights:
         copy.start()
@@ -102,27 +100,44 @@
     squares = jnp.sum(jnp.sum(x * x, axis=0, keepdims=True), axis=1, keepdims=True)
     inverse_rms = lax.rsqrt(squares / (C * LANES) + 1e-06)
     normed = (x * inverse_rms * gain_ref[...]).astype(jnp.bfloat16)
-    rows[r, z] = normed
+    rows[mine, z] = normed
 
     pl.semaphore_wait(barrier, len(peers) + 1)
 
-    def row_copy(rr, zz, send_sem, zp, rp):
+    def row_copy(k, zz, i, zp, rp):
         return pltpu.make_async_remote_copy(
-            src_ref=rows.at[rr, zz],
-            dst_ref=rows.at[rr, zz],
-            send_sem=send_sem,
-            recv_sem=ag_recv.at[rr, zz],
+            src_ref=rows.at[k, zz],
+            dst_ref=rows.at[k, zz],
+            send_sem=ag_send.at[i],
+            recv_sem=ag_recv.at[k, zz],
             device_id={"expert": zp, "replica": rp},
             device_id_type=MESH,
         )
 
     for i, zp, rp in reversed(peers):
-        row_copy(r, z, ag_send.at[i], zp, rp).start()
-    row_copy(r, z, ag_send.at[len(peers)], z, partner).start()
-
-    def spread(rr, zz):
-        at = pl.multiple_of((rr * Z + zz) * C, C)
-        flat[pl.ds(at, C), :] = rows[rr, zz].astype(jnp.float32)
+        row_copy(mine, z, i, zp, rp).start()
+
+    def share(j, src, dst):
+        return pltpu.make_async_remote_copy(
+            src_ref=src,
+            dst_ref=dst,
+            send_sem=share_send.at[j],
+            recv_sem=share_recv.at[j],
+            device_id={"replica": partner},
+            device_id_type=MESH,
+        )
+
+    shared = [
+        share(0, gate_ref.at[0], wgu.at[:, pl.ds(2 * F, F)]),
+        share(1, up_ref.at[0], wgu.at[:, pl.ds(3 * F, F)]),
+        share(2, down_ref.at[0], wd.at[pl.ds(F, F), :]),
+    ]
+    for copy in shared:
+        copy.start()
+
+    def spread(k, zz):
+        at = pl.multiple_of((k * Z + zz) * C, C)
+        flat[pl.ds(at, C), :] = rows[k, zz].astype(jnp.float32)
 
     small[2].wait()
     small[3].wait()
@@ -141,24 +156,29 @@
     chosen = members / (1.0 + jnp.exp(-logits))
     wts[...] = ROUTE_SCALE * chosen / jnp.sum(chosen, axis=0, keepdims=True)
 
-    spread(r, z)
+    spread(mine, z)
     for i, zp, rp in peers:
-        row_copy(rp, zp, ag_send.at[i], zp, rp).wait_recv()
-        row_copy(rp, zp, ag_pass.at[i], z, partner).start()
-        spread(rp, zp)
-    for i, zp, rp in [(len(peers), z, r)] + peers:
-        other = rp + partner - r
-        row_copy(other, zp, ag_send.at[i], z, partner).wait_recv()
-        spread(other, zp)
+        kp = lax.div(rp, 2)
+        row_copy(kp, zp, i, zp, rp).wait_recv()
+        spread(kp, zp)
     for c in range(C):
         lhs[:, pl.ds(c * LANES, LANES)] = flat[pl.ds(c, M, stride=C), :].astype(jnp.bfloat16)
+
+    def hidden_of(at):
+        gate_up = jnp.dot(
+            lhs[...], wgu[:, pl.ds(at, 2 * F)], preferred_element_type=jnp.float32
+        )
+        gate_act, up_act = gate_up[:, :F], gate_up[:, F:]
+        return (gate_act / (1.0 + jnp.exp(-gate_act)) * up_act).astype(jnp.bfloat16)
 
     weights[0].wait()
     weights[1].wait()
-    gate_up = jnp.dot(lhs[...], wgu[...], preferred_element_type=jnp.float32)
-    gate_act, up_act = gate_up[:, :F], gate_up[:, F:]
-    hidden = (gate_act / (1.0 + jnp.exp(-gate_act)) * up_act).astype(jnp.bfloat16)
+    own_hidden = hidden_of(0)
+    shared[0].wait_recv()
+    shared[1].wait_recv()
+    hidden = jnp.concatenate([own_hidden, hidden_of(2 * F)], axis=1)
     weights[2].wait()
+    shared[2].wait_recv()
     step = 4
     for n in range(C // step):
         piece = jnp.dot(
@@ -169,29 +189,9 @@
         for j in range(step):
             part[pl.ds(n * step + j, M, stride=C), :] = piece[:, j * LANES : (j + 1) * LANES]
 
-    span = Z * C
-    half = R // 2
-
-    def pair_copy(k):
-        return pltpu.make_async_remote_copy(
-            src_ref=psnd.at[k],
-            dst_ref=pgot.at[k],
-            send_sem=rs_psend.at[k],
-            recv_sem=rs_precv.at[k],
-            device_id={"replica": partner},
-            device_id_type=MESH,
-        )
-
-    mine_k = lax.div(r, 2)
-    order = [lax.div(flip(r, 2 * b), 2) for b in reversed(range(half))]
-    for k in order:
-        at = pl.multiple_of((2 * k + 1 - core) * span, span)
-        psnd[k] = part[pl.ds(at, span), :].astype(jnp.bfloat16)
-        pair_copy(k).start()
-
     def sum_copy(i, zp, rp, own):
         kp = lax.div(rp, 2)
-        slot = (mine_k, z) if own else (kp, zp)
+        slot = (mine, z) if own else (kp, zp)
         return pltpu.make_async_remote_copy(
             src_ref=snd.at[kp, zp],
             dst_ref=got.at[slot[0], slot[1]],
@@ -201,16 +201,14 @@
             device_id_type=MESH,
         )
 
-    for b in reversed(range(half)):
-        k = order[half - 1 - b]
-        pair_copy(k).wait_recv()
-        at = pl.multiple_of((2 * k + core) * span, span)
-        acc[...] = part[pl.ds(at, span), :] + pgot[k].astype(jnp.float32)
-        for (i, zp, rp), (_, bb) in reversed(list(zip(peers, pairs))):
-            if bb == 2 * b:
-                snd[k, zp] = acc[pl.ds(pl.multiple_of(zp * C, C), C), :].astype(jnp.bfloat16)
-                sum_copy(i, zp, rp, True).start()
-    total = acc[pl.ds(pl.multiple_of(z * C, C), C), :] * wts[pl.ds(z, 1), :]
+    def sums(k, zz):
+        return part[pl.ds(pl.multiple_of((k * Z + zz) * C, C), C), :]
+
+    for i, zp, rp in reversed(peers):
+        kp = lax.div(rp, 2)
+        snd[kp, zp] = sums(kp, zp).astype(jnp.bfloat16)
+        sum_copy(i, zp, rp, True).start()
+    total = sums(mine, z) * wts[pl.ds(z, 1), :]
     for i, zp, rp in peers:
         sum_copy(i, zp, rp, False).wait_recv()
         total += got[lax.div(rp, 2), zp].astype(jnp.float32) * wts[pl.ds(zp, 1), :]
@@ -222,12 +220,10 @@
         ).astype(jnp.bfloat16)
 
     for i, zp, rp in peers:
-        row_copy(r, z, ag_send.at[i], zp, rp).wait_send()
-        row_copy(rp, zp, ag_pass.at[i], z, partner).wait_send()
+        row_copy(mine, z, i, zp, rp).wait_send()
         sum_copy(i, zp, rp, True).wait_send()
-    row_copy(r, z, ag_send.at[len(peers)], z, partner).wait_send()
-    for k in order:
-        pair_copy(k).wait_send()
+    for copy in shared:
+        copy.wait_send()
 
 
 def solution(mesh):
@@ -237,7 +233,7 @@
         D = beam_rows.shape[1]
         F = gate_proj.shape[2]
         C = D // LANES
-        M = Z * R
+        M = Z * R // 2
         E = router.shape[1]
         vmem = pl.BlockSpec(memory_space=pltpu.VMEM)
         anywhere = pl.BlockSpec(memory_space=pl.ANY)
@@ -252,26 +248,22 @@
                 pltpu.VMEM((C, LANES), jnp.float32),
                 pltpu.VMEM((E, D), router.dtype),
                 pltpu.SMEM(routes.shape[::-1], jnp.int32),
-                pltpu.VMEM((D, 2 * F), jnp.bfloat16),
-                pltpu.VMEM((F, D), jnp.bfloat16),
+                pltpu.VMEM((D, 4 * F), jnp.bfloat16),
+                pltpu.VMEM((2 * F, D), jnp.bfloat16),
                 pltpu.VMEM((C, LANES), jnp.float32),
-                pltpu.VMEM((R, Z, C, LANES), jnp.bfloat16),
+                pltpu.VMEM((R // 2, Z, C, LANES), jnp.bfloat16),
                 pltpu.VMEM((M * C, LANES), jnp.float32),
                 pltpu.VMEM((M, D), jnp.bfloat16),
                 pltpu.VMEM((M * C, LANES), jnp.float32),
-                pltpu.VMEM((R // 2, Z * C, LANES), jnp.bfloat16),
-                pltpu.VMEM((R // 2, Z * C, LANES), jnp.bfloat16),
-                pltpu.VMEM((Z * C, LANES), jnp.float32),
                 pltpu.VMEM((R // 2, Z, C, LANES), jnp.bfloat16),
                 pltpu.VMEM((R // 2, Z, C, LANES), jnp.bfloat16),
                 pltpu.VMEM((E, LANES), jnp.float32),
                 dma((7,)),
-                dma((M // 2,)),
-                dma((M // 2,)),
-                dma((R, Z)),
-                dma((R // 2,)),
-                dma((R // 2,)),
-                dma((M // 2,)),
+                dma((M,)),
+                dma((R // 2, Z)),
+                dma((3,)),
+                dma((3,)),
+                dma((M,)),
                 dma((R // 2, Z)),
             ],
             compiler_params=pltpu.CompilerParams(

time: 23 us -> 20.9 us (0.909)
  Pallas kernels: 21.3 us -> 19.2 us
    pallas_call x1, Pallas kernels: 21.3 us -> 19.2 us  [on_device(): pl.pallas_call(functools.partial(moe_kernel, Z, R), out_shape=jax.ShapeDt...]
where the time goes in v4:
time: 20.9 us; the launch traced here: 20.6 us
  Pallas kernels  19.2 us (92%)
  local copies, waits for them, and re-layouts  1.34 us (6%)
    pallas_call x1, Pallas kernels, on_device(): pl.pallas_call(functools.partial(moe_kernel, Z, R), out_shape=jax.ShapeDt...  19.2 us
    unnamed x1, local copies, waits for them, and re-layouts  1.34 us

profile of v4, /device:TPU:0, one launch (start us, length us, event | category | flops | bytes accessed | tf_op | source)
XLA Modules:
  0.0 20.6 jit_solution(17468024881171802416)
XLA Ops:
  0.0 19.2 %shard_map.73 = bf16[1,4096]{1,0:T(2,128)(2,1)} custom-call(bf16[1,4096]{1,0:T(2,128)(2,1)} %x_hbm.1, f32[32,128]{1,0:T(8,128)} %bitcast.4, bf16[4,4096]{1,0:T(4,128)(2,1)} %bitcast.3, s32[2,8]{1,0:T(2,128)} %bitcast.5, bf16[1,4096,128]{2,1,0:T(8,128)(2,1)} %gate_ref.1, bf16[1,4096,128]{2,1,0:T(8,128)(2,1)} %up_ref.1, bf16[1,128,4096]{2,1,0:T(8,128)(2,1)} %down_ref.1), custom_call_target="tpu_custom_call" | custom-call | tf_op jit(solution)/shard_map/pallas_call | solution.py:241
  19.2 1.3 %copy.9 = bf16[1,4096]{1,0:T(2,128)(2,1)} copy(bf16[1,4096]{1,0:T(2,128)(2,1)} %shard_map.73) | data formatting | bytes 16384

commit v5 on v4

--- a/solution.py
+++ b/solution.py
@@ -164,20 +164,14 @@
     for c in range(C):
         lhs[:, pl.ds(c * LANES, LANES)] = flat[pl.ds(c, M, stride=C), :].astype(jnp.bfloat16)
 
-    def hidden_of(at):
-        gate_up = jnp.dot(
-            lhs[...], wgu[:, pl.ds(at, 2 * F)], preferred_element_type=jnp.float32
-        )
-        gate_act, up_act = gate_up[:, :F], gate_up[:, F:]
-        return (gate_act / (1.0 + jnp.exp(-gate_act)) * up_act).astype(jnp.bfloat16)
-
-    weights[0].wait()
-    weights[1].wait()
-    own_hidden = hidden_of(0)
+    for copy in weights:
+        copy.wait()
     shared[0].wait_recv()
     shared[1].wait_recv()
-    hidden = jnp.concatenate([own_hidden, hidden_of(2 * F)], axis=1)
-    weights[2].wait()
+    acts = jnp.dot(lhs[...], wgu[...], preferred_element_type=jnp.float32)
+    gates = jnp.concatenate([acts[:, :F], acts[:, 2 * F : 3 * F]], axis=1)
+    ups = jnp.concatenate([acts[:, F : 2 * F], acts[:, 3 * F :]], axis=1)
+    hidden = (gates / (1.0 + jnp.exp(-gates)) * ups).astype(jnp.bfloat16)
     shared[2].wait_recv()
     step = 4
     for n in range(C // step):
@@ -208,22 +202,19 @@
         kp = lax.div(rp, 2)
         snd[kp, zp] = sums(kp, zp).astype(jnp.bfloat16)
         sum_copy(i, zp, rp, True).start()
-    total = sums(mine, z) * wts[pl.ds(z, 1), :]
-    for i, zp, rp in peers:
-        sum_copy(i, zp, rp, False).wait_recv()
-        total += got[lax.div(rp, 2), zp].astype(jnp.float32) * wts[pl.ds(zp, 1), :]
-
-    for c in range(C):
-        lane = pl.ds(c * LANES, LANES)
-        out_ref[:, lane] = (
-            x_ref[:, lane].astype(jnp.float32) + total[c : c + 1, :]
-        ).astype(jnp.bfloat16)
-
     for i, zp, rp in peers:
         row_copy(mine, z, i, zp, rp).wait_send()
         sum_copy(i, zp, rp, True).wait_send()
     for copy in shared:
         copy.wait_send()
+    total = sums(mine, z) * wts[pl.ds(z, 1), :]
+    for i, zp, rp in peers:
+        sum_copy(i, zp, rp, False).wait_recv()
+        total += got[lax.div(rp, 2), zp].astype(jnp.float32) * wts[pl.ds(zp, 1), :]
+
+    xs[...] = x + total
+    for c in range(C):
+        out_ref[:, pl.ds(c * LANES, LANES)] = xs[pl.ds(c, 1), :].astype(jnp.bfloat16)
 
 
 def solution(mesh):

time: 20.9 us -> 20.5 us (0.981)
  Pallas kernels: 19.2 us -> 18.8 us
    pallas_call x1, Pallas kernels: 19.2 us -> 18.8 us  [on_device(): pl.pallas_call(functools.partial(moe_kernel, Z, R), out_shape=jax.ShapeDt...]
where the time goes in v5:
time: 20.5 us; the launch traced here: 20.1 us
  Pallas kernels  18.8 us (92%)
  local copies, waits for them, and re-layouts  1.34 us (7%)
    pallas_call x1, Pallas kernels, on_device(): pl.pallas_call(functools.partial(moe_kernel, Z, R), out_shape=jax.ShapeDt...  18.8 us
    unnamed x1, local copies, waits for them, and re-layouts  1.34 us

profile of v5, /device:TPU:0, one launch (start us, length us, event | category | flops | bytes accessed | tf_op | source)
XLA Modules:
  0.0 20.1 jit_solution(15762234179685860347)
XLA Ops:
  0.0 18.8 %shard_map.73 = bf16[1,4096]{1,0:T(2,128)(2,1)} custom-call(bf16[1,4096]{1,0:T(2,128)(2,1)} %x_hbm.1, f32[32,128]{1,0:T(8,128)} %bitcast.4, bf16[4,4096]{1,0:T(4,128)(2,1)} %bitcast.3, s32[2,8]{1,0:T(2,128)} %bitcast.5, bf16[1,4096,128]{2,1,0:T(8,128)(2,1)} %gate_ref.1, bf16[1,4096,128]{2,1,0:T(8,128)(2,1)} %up_ref.1, bf16[1,128,4096]{2,1,0:T(8,128)(2,1)} %down_ref.1), custom_call_target="tpu_custom_call" | custom-call | tf_op jit(solution)/shard_map/pallas_call | solution.py:232
  18.8 1.3 %copy.9 = bf16[1,4096]{1,0:T(2,128)(2,1)} copy(bf16[1,4096]{1,0:T(2,128)(2,1)} %shard_map.73) | data formatting | bytes 16384
